TPU v7x, 128 devices: a whole 4x4x4 slice. The times are simulated.
128 devices in a mesh: db: 32 (over z, y, core), sub: 4 (over x).
Axes of the slice: x: 4, y: 4, z: 4, core: 2. Of those that a mesh axis runs over, the one named last changes fastest.
Arguments:
- codes: int32 [32768, 64], P('db', 'sub'), may hold values from 0 to 255
- tables: bfloat16 [2048, 64, 256], P('db', 'sub'), may hold values from 0.125 to 128, as said below
- limits: int32 [2048], replicated, may hold values from 3008 to 3263
Outputs:
- hit_ids: int32 [2048, 128], P(('db', 'sub'))
- hit_count: int32 [2048], P(('db', 'sub'))
Inputs may be any that keep to these rules, and one draw needn't show every extreme that they name: `tables`: each value is a bfloat16 number of at least 1/8 and at most 128.
All inputs are finite; a program needn't handle non-finite values.
Results may differ from a plain program's by a relative error of at most 0.000001.
Values may be sent and summed in bfloat16 or wider, within the bound.
No kernel may reach another device: no remote copies, remote signals or barrier semaphores. Data moves between devices by JAX's collectives and lax.ppermute only.
A program may use at most 128 MiB of HBM per device.

v0:
```python
import math

import jax
import jax.numpy as jnp
from jax import lax
from jax.sharding import PartitionSpec as P

K = 256
SLOTS = 128
QB = 16


def copy_for_each(shard, axis):
    copies = jnp.broadcast_to(shard, (lax.axis_size(axis), *shard.shape))
    return lax.all_to_all(copies, axis, split_axis=0, concat_axis=0, tiled=True)


def in_order(tiles, dim):
    tiles = jnp.moveaxis(tiles, 0, dim)
    shape = tiles.shape
    return tiles.reshape(*shape[:dim], shape[dim] * shape[dim + 1], *shape[dim + 2 :])


def collect(shard, axis, dim):
    tiles = copy_for_each(shard, axis)
    return in_order(tiles, dim)


def folded_in_pairs(pieces, combine):
    while len(jax.tree.leaves(pieces)[0]) > 1:
        pieces = jax.vmap(combine)(*(pieces[side::2] for side in (0, 1)))
    return pieces[0]


def carried_in(shard, axis, combine, identity):
    devices, position = (lax.axis_size(axis), lax.axis_index(axis))
    passed = jnp.arange(devices) < position

    def kept(part, zero, own):
        part = jnp.where(
            passed.reshape(-1, *(1 for _ in own.shape)), part, jnp.asarray(zero, own.dtype)
        )
        return part

    pieces = copy_for_each(shard, axis)
    return folded_in_pairs(kept(pieces, identity, shard), combine)


def in_one_piece(arrays, axis, split_dim, concat_dim, along):
    widths = [math.prod(a.shape[along:]) for a in arrays]
    both = jnp.concatenate(
        [a.reshape(*a.shape[:along], w) for a, w in zip(arrays, widths)], axis=along
    )
    whole = lax.all_to_all(both, axis, split_axis=split_dim, concat_axis=concat_dim, tiled=True)
    tiles = jnp.split(whole, [sum(widths[:k]) for k in range(1, len(widths))], axis=along)
    return tuple((b.reshape(*whole.shape[:along], *a.shape[along:]) for a, b in zip(arrays, tiles)))


def one_hot_codes(group_codes):
    width = group_codes.shape[1]
    centroid = lax.iota(jnp.int32, K)
    table = group_codes.T[:, None, :] == centroid[None, :, None]
    return table.astype(jnp.bfloat16).reshape(width * K, group_codes.shape[0])


def pack_codes(group_codes):
    row_count = group_codes.shape[0]
    quads = group_codes.reshape(row_count, group_codes.shape[1] // 4, 4)
    packed_words = quads[:, :, 0]
    packed_words = jnp.bitwise_or(packed_words, jnp.left_shift(quads[:, :, 1], 8))
    packed_words = jnp.bitwise_or(packed_words, jnp.left_shift(quads[:, :, 2], 16))
    packed_words = jnp.bitwise_or(packed_words, jnp.left_shift(quads[:, :, 3], 24))
    return packed_words


def unpack_codes(packed_words):
    row_count = packed_words.shape[0]
    shifts = 8 * lax.iota(jnp.int32, 4)
    opened = jnp.bitwise_and(jnp.right_shift(packed_words[:, :, None], shifts[None, None, :]), 255)
    return opened.reshape(row_count, packed_words.shape[1] * 4)


def list_hits(operands):
    running_block, matched_block, wanted_block = operands
    position = lax.iota(jnp.int32, running_block.shape[1])
    equal = (running_block[:, None, :] == wanted_block[:, :, None] + 1.0) & matched_block[
        :, None, :
    ]
    return jnp.sum(jnp.where(equal, position[None, None, :], 0), axis=2, dtype=jnp.int32)


def per_device(codes, tables, limits):
    row_count = codes.shape[0]
    groups = lax.axis_size("db")
    parts = lax.axis_size("sub")
    db_index = lax.axis_index("db")
    sub_index = lax.axis_index("sub")
    tables_flat = tables.reshape(tables.shape[0], -1)
    gathered_words = collect(pack_codes(codes), "sub", 1)
    all_codes = unpack_codes(gathered_words)
    own_queries = lax.all_to_all(tables_flat, "sub", split_axis=0, concat_axis=1, tiled=True)
    query_tables = lax.all_gather(own_queries, "db", axis=0, tiled=True)
    group_width = codes.shape[1]
    span = group_width * K
    distance = jnp.zeros((query_tables.shape[0], row_count), jnp.float32)
    for group in range(parts):
        encoded = one_hot_codes(all_codes[:, group * group_width : (group + 1) * group_width])
        distance = distance + jnp.dot(
            query_tables[:, group * span : (group + 1) * span],
            encoded,
            preferred_element_type=jnp.float32,
        )
    distance = distance.reshape(groups, QB, row_count)
    limit_mine = lax.dynamic_index_in_dim(
        limits.reshape(groups, parts, QB), sub_index, 1, keepdims=False
    ).astype(jnp.float32)
    matched = distance <= limit_mine[..., None]
    counts = jnp.sum(matched, axis=2, dtype=jnp.int32)
    flags = matched.astype(jnp.bfloat16).reshape(groups * QB, row_count)
    position = lax.iota(jnp.int32, row_count)
    upper = (position[:, None] <= position[None, :]).astype(jnp.bfloat16)
    running = jnp.dot(flags, upper, preferred_element_type=jnp.float32).reshape(
        groups, QB, row_count
    )
    slot_index = lax.iota(jnp.int32, SLOTS)
    first_id = db_index * row_count + 1
    offsets = carried_in(
        counts, "db", lambda earlier, later: earlier + later, jnp.zeros_like(counts)
    )
    wanted = slot_index[None, None, :] - offsets[..., None]
    valid = (wanted >= 0) & (wanted < counts[..., None])
    listed = lax.map(list_hits, (running, matched, wanted.astype(jnp.float32)))
    sent = jnp.where(valid, listed + first_id, 0)
    received, source_counts = in_one_piece((sent, counts), "db", 0, 0, 2)
    hit_count = jnp.sum(source_counts, axis=0)
    placed = jnp.sum(received, axis=0)
    return (placed - 1, hit_count)


def solution(mesh):
    placed = (P("db", "sub"), P("db", "sub", None), P())
    return jax.shard_map(
        per_device,
        mesh=mesh,
        in_specs=placed,
        out_specs=(P(("db", "sub"), None), P(("db", "sub"))),
        check_vma=False,
    )
```

profile of v0, /device:TPU:0, one launch (start us, length us, event | category | flops | bytes accessed | tf_op | source)
XLA Modules:
  0.0 272.7 jit_solution(4565977795853774773)
XLA Ops:
  8.5 13.7 %all_to_all.34 = bf16[4,16,4096]{2,1,0:T(8,128)(2,1)S(1)} all-to-all(bf16[4,16,4096]{2,1,0:T(8,128)(2,1)S(1)} %all_to_all.24), channel_id=1, replica_groups=mesh['db'=32,'sub'=4] {'sub'}, dimensions={0} | all-to-all | bytes 1048576 | tf_op jit(solution)/shard_map/all_to_all | solution.py:101
  24.6 3.3 %all-to-all-start = ((s32[4,1024,4]{1,2,0:T(4,128)}), s32[4,1024,4]{1,2,0:T(4,128)S(1)}, u32[]{:S(2)}, u32[]{:S(2)}) async-start(s32[4,1024,4]{1,2,0:T(4,128)} %broadcast_in_dim.31), calls=%async_computation | async-start | bytes 131072 | tf_op jit(solution)/shard_map/all_to_all | solution.py:15
  30.1 3.3 %all-to-all-done = s32[4,1024,4]{1,2,0:T(4,128)S(1)} async-done(((s32[4,1024,4]{1,2,0:T(4,128)}), s32[4,1024,4]{1,2,0:T(4,128)S(1)}, u32[]{:S(2)}, u32[]{:S(2)}) %all-to-all-start) | async-done | bytes 65568 | tf_op jit(solution)/shard_map/all_to_all | solution.py:15
  33.8 12.1 %bitcast_compare_fusion.3 = (pred[4096,1024]{1,0:T(32,128)(4,1)}, pred[4096,1024]{1,0:T(32,128)(4,1)}, pred[4096,1024]{1,0:T(32,128)(4,1)}, pred[4096,1024]{1,0:T(32,128)(4,1)}) fusion(s32[4096]{0:T(1024)S(1)} %bitcast.78, s32[16,1024]{1,0:T(8,128)S(1)} %get-tuple-element.44, s32[16,1024]{1,0:T(8,128)S(1)} %get-tuple-element.47, ...), kind=kLoop, calls=%fused_computation.8 | loop fusion | flops 16777216 | bytes 17055744 | tf_op jit(solution)/shard_map/eq | solution.py:62
  45.8 50.5 %all-gather.2.cloned.1.call-done = bf16[512,16384]{1,0:T(8,128)(2,1)} async-done(((bf16[16,16384]{1,0:T(8,128)(2,1)}), bf16[512,16384]{1,0:T(8,128)(2,1)}) %all-gather.2.cloned.1.call-update) | async-done | bytes 16777232 | tf_op jit(solution)/shard_map/all_gather | solution.py:102
  96.3 7.7 %fusion = f32[1024,512]{0,1:T(8,128)S(1)} fusion(pred[4096,1024]{1,0:T(32,128)(4,1)} %get-tuple-element.51, bf16[512,16384]{1,0:T(8,128)(2,1)} %all-gather.2.cloned.1.call-done), kind=kOutput, calls=%fused_computation.9 | convolution fusion | flops 4294967296 | bytes 10485760 | tf_op jit(solution)/shard_map/dot_general | solution.py:108
  104.1 6.8 %fusion.2 = f32[1024,512]{0,1:T(8,128)S(1)} fusion(pred[4096,1024]{1,0:T(32,128)(4,1)S(1)} %copy-done.2, bf16[512,16384]{1,0:T(8,128)(2,1)} %all-gather.2.cloned.1.call-done), kind=kOutput, calls=%fused_computation.11 | convolution fusion | flops 4294967296 | bytes 10485760 | tf_op jit(solution)/shard_map/dot_general | solution.py:108
  110.9 8.2 %fusion.4 = f32[1024,512]{0,1:T(8,128)} fusion(pred[4096,1024]{1,0:T(32,128)(4,1)S(1)} %copy-done.1, bf16[512,16384]{1,0:T(8,128)(2,1)} %all-gather.2.cloned.1.call-done), kind=kOutput, calls=%fused_computation.13 | convolution fusion | flops 4294967296 | bytes 10485760 | tf_op jit(solution)/shard_map/dot_general | solution.py:108
  119.1 8.7 %convert_reduce_fusion = (s32[512]{0:T(512)S(1)}, pred[512,1024]{1,0:T(8,128)(4,1)}, f32[1024,512]{0,1:T(8,128)S(1)}) fusion(f32[512]{0:T(512)S(1)} %convert_element_type.28, f32[1024,512]{0,1:T(8,128)S(1)} %fusion, f32[1024,512]{0,1:T(8,128)S(1)} %fusion.2, f32[1024,512]{0,1:T(8,128)} %fusion.4, pred[4096,1024]{1,0:T(32,128)(4,1)S(1)} %copy-done, ...), kind=kOutput, calls=%fused_computation.21 | convolution fusion | flops 4298112512 | bytes 17305600 | tf_op jit(solution)/shard_map/dot_general | solution.py:108
  128.7 5.6 %all-to-all-start.2 = ((s32[32,1,512]{2,1,0:T(1,128)}), s32[32,1,512]{2,1,0:T(1,128)S(1)}, u32[]{:S(2)}, u32[]{:S(2)}) async-start(s32[32,1,512]{2,1,0:T(1,128)} %reshape.104), calls=%async_computation.2 | async-start | bytes 131072 | tf_op jit(solution)/shard_map/all_to_all | solution.py:15
  134.4 3.7 %fusion.9 = f32[32,16,1024]{2,1,0:T(8,128)} fusion(pred[32,16,1024]{2,1,0:T(8,128)(4,1)} %bitcast.80), kind=kOutput, calls=%fused_computation.19 | convolution fusion | flops 1074790400 | bytes 2621440 | tf_op jit(solution)/shard_map/dot_general | solution.py:122
  138.6 3.0 %all-to-all-done.2 = s32[32,1,512]{2,1,0:T(1,128)S(1)} async-done(((s32[32,1,512]{2,1,0:T(1,128)}), s32[32,1,512]{2,1,0:T(1,128)S(1)}, u32[]{:S(2)}, u32[]{:S(2)}) %all-to-all-start.2) | async-done | bytes 65568 | tf_op jit(solution)/shard_map/all_to_all | solution.py:15
  143.5 105.1 %while.11 = (s32[]{:T(128)}, s32[32,16,128]{2,1,0:T(8,128)S(1)}, f32[32,16,1024]{2,1,0:T(8,128)}, f32[32,16,128]{2,1,0:T(8,128)S(1)}, pred[32,16,1024]{2,1,0:T(8,128)(4,1)S(1)}) while((s32[]{:T(128)}, s32[32,16,128]{2,1,0:T(8,128)S(1)}, f32[32,16,1024]{2,1,0:T(8,128)}, f32[32,16,128]{2,1,0:T(8,128)S(1)}, ...), condition=%wide.region_3.4_spmd.clone, body=%wide.region_1.3_spmd.sunk.clone | while | flops 8388610 | bytes 294989 | solution.py:132
  147.6 2.4 select_reduce_fusion.3
  150.9 2.4 select_reduce_fusion.3
  154.2 2.4 select_reduce_fusion.3
  160.7 2.4 select_reduce_fusion.3
  164.0 2.4 select_reduce_fusion.3
  167.3 2.4 select_reduce_fusion.3
  170.6 2.4 select_reduce_fusion.3
  177.2 2.4 select_reduce_fusion.3
  180.4 2.4 select_reduce_fusion.3
  183.7 2.4 select_reduce_fusion.3
  187.0 2.4 select_reduce_fusion.3
  193.6 2.4 select_reduce_fusion.3
  196.9 2.4 select_reduce_fusion.3
  200.2 2.4 select_reduce_fusion.3
  210.0 2.4 select_reduce_fusion.3
  213.3 2.4 select_reduce_fusion.3
  216.6 2.4 select_reduce_fusion.3
  223.1 2.4 select_reduce_fusion.3
  248.8 15.7 %all_to_all.35 = s32[32,16,129]{2,1,0:T(8,128)S(1)} all-to-all(s32[32,16,129]{2,1,0:T(8,128)S(1)} %pad_add_fusion), channel_id=1, replica_groups=mesh['db'=32,'sub'=4] {'db'}, dimensions={0} | all-to-all | bytes 528384 | tf_op jit(solution)/shard_map/all_to_all | solution.py:54
  (194 shorter events, 72.1 us)
Async XLA Ops:
  7.2 89.2 %all-gather.2.cloned.1.call-start = ((), (), s32[]{:S(2)}) async-start(), calls=%async_computation.4 | async-start | bytes 17301504 | tf_op jit(solution)/shard_map/all_gather | solution.py:102
  24.6 8.9 %all-to-all-start = ((s32[4,1024,4]{1,2,0:T(4,128)}), s32[4,1024,4]{1,2,0:T(4,128)S(1)}, u32[]{:S(2)}, u32[]{:S(2)}) async-start(s32[4,1024,4]{1,2,0:T(4,128)} %broadcast_in_dim.31), calls=%async_computation | async-start | bytes 131072 | tf_op jit(solution)/shard_map/all_to_all | solution.py:15
  96.3 7.7 %copy-start.2 = (pred[4096,1024]{1,0:T(32,128)(4,1)S(1)}, pred[4096,1024]{1,0:T(32,128)(4,1)}, u32[]{:S(2)}) copy-start(pred[4096,1024]{1,0:T(32,128)(4,1)} %get-tuple-element.50) | copy-start | bytes 12582916
  104.1 6.8 %copy-start.1 = (pred[4096,1024]{1,0:T(32,128)(4,1)S(1)}, pred[4096,1024]{1,0:T(32,128)(4,1)}, u32[]{:S(2)}) copy-start(pred[4096,1024]{1,0:T(32,128)(4,1)} %get-tuple-element.49) | copy-start | bytes 12582916
  110.9 8.2 %copy-start = (pred[4096,1024]{1,0:T(32,128)(4,1)S(1)}, pred[4096,1024]{1,0:T(32,128)(4,1)}, u32[]{:S(2)}) copy-start(pred[4096,1024]{1,0:T(32,128)(4,1)} %get-tuple-element.48) | copy-start | bytes 12582916
  128.7 12.9 %all-to-all-start.2 = ((s32[32,1,512]{2,1,0:T(1,128)}), s32[32,1,512]{2,1,0:T(1,128)S(1)}, u32[]{:S(2)}, u32[]{:S(2)}) async-start(s32[32,1,512]{2,1,0:T(1,128)} %reshape.104), calls=%async_computation.2 | async-start | bytes 131072 | tf_op jit(solution)/shard_map/all_to_all | solution.py:15
Sparse Core Ops, SparseCore 0:
  23.1 73.1 all-gather.1
where the time goes:
time: 276 us; the launch traced here: 273 us
  other arithmetic  92.4 us (33%)
  waiting for transfers between devices  56.8 us (21%)
  matrix products  35 us (13%)
  local copies, waits for them, and re-layouts  34.7 us (13%)
  blocking collectives  29.4 us (11%)
  between operations  14.3 us (5%)
  starting transfers between devices  8.94 us (3%)
    reduce_sum x32, other arithmetic, list_hits(): jnp.sum(jnp.where(equal, position[None, None, :], 0), axis=2, dtype=jnp.i...  76.4 us
    all_gather x1, waiting for transfers between devices, per_device(): query_tables = lax.all_gather(own_queries, 'db', axis=0, tiled=True)  50.5 us
    dot_general x4, matrix products, per_device(): jnp.dot(query_tables[:, group * span:(group + 1) * span], encoded, prefer...  31.4 us
    eq x32, local copies, waits for them, and re-layouts, list_hits(): running_block[:, None, :] == wanted_block[:, :, None] + 1.0  27.2 us
    all_to_all x1, blocking collectives, in_one_piece(): lax.all_to_all(both, axis, split_axis=split_dim, concat_axis=concat_dim,...  15.7 us
    all_to_all x1, blocking collectives, per_device(): lax.all_to_all(tables_flat, 'sub', split_axis=0, concat_axis=1, tiled=True)  13.7 us
    eq x1, other arithmetic, one_hot_codes(): table = group_codes.T[:, None, :] == centroid[None, :, None]  12.1 us
    all_to_all x2, starting transfers between devices, copy_for_each(): return lax.all_to_all(copies, axis, split_axis=0, concat_axis=0, tiled=True)  8.9 us
  transfers between devices with their start and end apart: 3, of which 3 were waited for; matrix products, arithmetic and copies ran while one was open for 7% of the time, Pallas kernels for 0%

commit v1 on v0

v1 whole, which is shorter than its diff:
```python
import functools

import jax
import jax.numpy as jnp
from jax import lax
from jax.experimental import pallas as pl
from jax.experimental.pallas import tpu as pltpu
from jax.sharding import PartitionSpec as P

F8 = jnp.float8_e4m3fn
RANGES = 32
PARTS = 4
ROWS = 1024
QN = 64
QB = 16
K = 256
SLICE = ROWS // PARTS
CHUNK = 1024
GROUP = 8
LANES = 128
LOW_HALVES = {16: 0x0000FFFF, 8: 0x00FF00FF, 4: 0x0F0F0F0F, 2: 0x33333333, 1: 0x55555555}


def srl(word, by):
    return lax.shift_right_logical(word, jnp.full_like(word, by))


def popcount(word):
    word = word - (srl(word, 1) & 0x55555555)
    word = (word & 0x33333333) + (srl(word, 2) & 0x33333333)
    word = (word + srl(word, 4)) & 0x0F0F0F0F
    word = word + srl(word, 8)
    word = word + srl(word, 16)
    return word & 63


def lane_iota(rows):
    return lax.broadcasted_iota(jnp.int32, (rows, LANES), 1)


def picked(table, index):
    return jnp.take_along_axis(table, index, axis=1, mode="promise_in_bounds")


def exact_dot(a, b):
    return jnp.dot(
        a.astype(jnp.float32).astype(jnp.bfloat16),
        b.astype(jnp.float32).astype(jnp.bfloat16),
        preferred_element_type=jnp.float32,
    )


def pack_kernel(codes_ref, out_ref):
    rows = lax.broadcasted_iota(jnp.int32, (8, 16), 0)
    cols = lax.broadcasted_iota(jnp.int32, (8, 16), 1)
    first = 4 * (rows % 4) + 2 * (rows // 4)
    weights = jnp.where(cols == first, 1.0, jnp.where(cols == first + 1, 256.0, 0.0))
    pairs = lax.dot_general(
        weights.astype(jnp.bfloat16),
        codes_ref[...].astype(jnp.float32).astype(jnp.bfloat16),
        (((1,), (1,)), ((), ())),
        preferred_element_type=jnp.float32,
    ).astype(jnp.int32)
    words = pairs[:4] | (pairs[4:] << 16)
    pieces = []
    for part in range(PARTS):
        for word in range(4):
            for block in range(2):
                at = part * SLICE + block * LANES
                pieces.append(words[word : word + 1, at : at + LANES])
    packed = jnp.concatenate(pieces, axis=0)
    for copy in range(RANGES):
        out_ref[copy] = packed


def split_tables(tab_refs, wide_ref, hl_ref):
    for quarter, tab_ref in enumerate(tab_refs):
        wide = tab_ref[...].astype(jnp.float32).reshape(QN * 16, K)
        for side in range(2):
            wide_ref[side] = wide[:, side * LANES : (side + 1) * LANES]
        for m in range(16):
            for side in range(2):
                value = wide_ref[side, pl.ds(m, QN, stride=16), :]
                hi = value.astype(F8)
                lo = ((value - hi.astype(jnp.float32)) * 8.0).astype(F8)
                at = (quarter * 16 + m) * K + side * LANES
                hl_ref[0:QN, at : at + LANES] = hi
                hl_ref[QN : 2 * QN, at : at + LANES] = lo


def one_hot_group(words_ref, onehot_ref, chunk, quarter, first_word):
    centroid = lax.broadcasted_iota(jnp.int32, (K, LANES), 0).astype(jnp.int8)
    for block in range(CHUNK // LANES):
        source = (chunk * (CHUNK // SLICE) + block // 2) * PARTS + quarter
        for word in range(GROUP // 4):
            row = words_ref[source, pl.ds((first_word + word) * 2 + block % 2, 1), :]
            row = jnp.broadcast_to(row, (32, LANES))
            for byte in range(4):
                code = ((row >> (8 * byte)) & 255).astype(jnp.int8)
                code = jnp.concatenate([code] * (K // 32), axis=0)
                at = (word * 4 + byte) * K
                onehot_ref[at : at + K, block * LANES : (block + 1) * LANES] = jnp.where(
                    code == centroid, F8(1), F8(0)
                )


def list_hits(bits_ref, position, out_ref):
    lane = lane_iota(QN)
    halves = []
    for half in range(2):
        word = bits_ref[half]
        for step, low in LOW_HALVES.items():
            high = low << step
            high = high - (1 << 32) if high >= (1 << 31) else high
            after = pltpu.roll(word, LANES - step, 1)
            before = pltpu.roll(word, step, 1)
            word = jnp.where(
                (lane & step) == 0,
                (word & low) | ((after & low) << step),
                (word & high) | srl(before & high, step),
            )
        halves.append(word)
    counts = [popcount(word) for word in halves]
    source = lax.broadcasted_iota(jnp.int32, (LANES, LANES), 0)
    target = lax.broadcasted_iota(jnp.int32, (LANES, LANES), 1)
    order = 4 * (source % 32) + source // 32
    upto = (order <= target).astype(jnp.float32)
    sums = [exact_dot(count, upto).astype(jnp.int32) for count in counts]
    per_range = sum(
        exact_dot(counts[half], (half * 16 + order // 8 == target).astype(jnp.float32))
        for half in range(2)
    )
    first_total = jnp.broadcast_to(sums[0][:, LANES - 1 :], (QN, LANES))
    second = lane >= first_total
    base = jnp.where(second, first_total, 0)
    wanted = lane - base
    found = jnp.zeros((QN, LANES), jnp.int32)
    base = jnp.zeros((QN, LANES), jnp.int32)
    for step in (64, 32, 16, 8, 4, 2, 1):
        index = found + (step - 1)
        count = jnp.where(second, picked(sums[1], index), picked(sums[0], index))
        passed = count <= wanted
        found = jnp.where(passed, found + step, found)
        base = jnp.where(passed, count, base)
    at = 32 * (found & 3) + (found >> 2)
    word = jnp.where(second, picked(halves[1], at), picked(halves[0], at))
    rank = wanted - base
    bit = jnp.zeros((QN, LANES), jnp.int32)
    for step in (16, 8, 4, 2, 1):
        count = popcount(word & ((1 << step) - 1))
        passed = count <= rank
        rank = jnp.where(passed, rank - count, rank)
        word = jnp.where(passed, srl(word, step), word)
        bit = jnp.where(passed, bit + step, bit)
    local = jnp.where(second, 4096, 0) + 32 * found + bit
    ids = (local >> 8) * ROWS + position * SLICE + (local & (SLICE - 1))
    out_ref[:, :LANES] = ids
    out_ref[:, LANES:] = per_range.astype(jnp.int32)


def score_kernel(
    where_ref, limits_ref, words_ref, t0, t1, t2, t3, out_ref, wide_ref, hl_ref, onehot_ref, bits_ref
):
    db, sub = where_ref[0], where_ref[1]
    split_tables((t0, t1, t2, t3), wide_ref, hl_ref)
    lane = lane_iota(QN)
    mine = 64 * (db % 2) + lax.broadcasted_iota(jnp.int32, (QN, LANES), 0)
    row = jnp.broadcast_to(limits_ref[pl.ds(db // 2, 1), :], (QN, LANES)).astype(jnp.float32)
    limit = jnp.sum(jnp.where(lane == mine, row, 0.0), axis=1, keepdims=True)
    limit = jnp.broadcast_to(limit, (QN, LANES))
    bits_ref[...] = jnp.zeros_like(bits_ref)

    def score(chunk, carry):
        total = jnp.zeros((2 * QN, CHUNK), jnp.float32)
        for group in range(64 // GROUP):
            quarter = (sub + PARTS - group // 2) % PARTS
            one_hot_group(words_ref, onehot_ref, chunk, quarter, (group % 2) * (GROUP // 4))
            at = group * GROUP * K
            total = total + jnp.dot(
                hl_ref[:, at : at + GROUP * K],
                onehot_ref[...],
                preferred_element_type=jnp.float32,
            )
        distance = total[:QN] + total[QN:] * 0.125
        bits = jnp.zeros((QN, LANES), jnp.int32)
        for block in range(CHUNK // LANES):
            matched = distance[:, block * LANES : (block + 1) * LANES] <= limit
            bits = bits | jnp.where(matched, 1 << block, 0)
        half = chunk // 4
        bits_ref[half] = bits_ref[half] | (bits << (8 * (chunk % 4)))
        return carry

    lax.fori_loop(0, RANGES * SLICE // CHUNK, score, 0)
    list_hits(bits_ref, sub, out_ref)


def merge_kernel(lists_ref, ids_ref, count_ref):
    lane = lane_iota(QB)
    source = lax.broadcasted_iota(jnp.int32, (LANES, LANES), 0)
    segment = lax.broadcasted_iota(jnp.int32, (LANES, LANES), 1)
    lists = [lists_ref[pl.ds(x * QB, QB), :LANES] for x in range(PARTS)]
    counts = [lists_ref[pl.ds(x * QB, QB), LANES:] for x in range(PARTS)]
    ends = jnp.zeros((QB, LANES), jnp.float32)
    skipped = jnp.zeros((QB, LANES), jnp.float32)
    totals = jnp.zeros((8, QB), jnp.float32)
    for x in range(PARTS):
        upto = (4 * source + x <= segment).astype(jnp.float32)
        ends = ends + exact_dot(counts[x], upto)
        ahead = ((segment % 4 == x) & (source < segment // 4)).astype(jnp.float32)
        skipped = skipped + exact_dot(counts[x], ahead)
        totals = totals + lax.dot_general(
            jnp.ones((8, LANES), jnp.bfloat16),
            counts[x].astype(jnp.float32).astype(jnp.bfloat16),
            (((1,), (1,)), ((), ())),
            preferred_element_type=jnp.float32,
        )
    ends = ends.astype(jnp.int32)
    skipped = skipped.astype(jnp.int32)
    found = jnp.zeros((QB, LANES), jnp.int32)
    base = jnp.zeros((QB, LANES), jnp.int32)
    for step in (64, 32, 16, 8, 4, 2, 1):
        count = picked(ends, found + (step - 1))
        passed = count <= lane
        found = jnp.where(passed, found + step, found)
        base = jnp.where(passed, count, base)
    valid = lane < jnp.broadcast_to(ends[:, LANES - 1 :], (QB, LANES))
    index = lane - base + picked(skipped, found)
    index = jnp.where(valid, index, 0)
    value = jnp.zeros((QB, LANES), jnp.int32)
    for x in range(PARTS):
        value = jnp.where(found % 4 == x, picked(lists[x], index), value)
    ids_ref[...] = jnp.where(valid, value, -1)
    count_ref[...] = totals[:1].astype(jnp.int32)


VMEM = pl.BlockSpec(memory_space=pltpu.VMEM)
SMEM = pl.BlockSpec(memory_space=pltpu.SMEM)
PARAMS = pltpu.CompilerParams(vmem_limit_bytes=48 * 2**20)


def pack(codes):
    return pl.pallas_call(
        pack_kernel,
        out_shape=jax.ShapeDtypeStruct((RANGES, PARTS * 8, LANES), jnp.int32),
        in_specs=[VMEM],
        out_specs=VMEM,
        compiler_params=PARAMS,
        name="pack",
    )(codes)


def score(where, limits, words, tabs):
    return pl.pallas_call(
        score_kernel,
        out_shape=jax.ShapeDtypeStruct((QN, 2 * LANES), jnp.int32),
        in_specs=[SMEM] + [VMEM] * 6,
        out_specs=VMEM,
        scratch_shapes=[
            pltpu.VMEM((2, QN * 16, LANES), jnp.float32),
            pltpu.VMEM((2 * QN, 64 * K), F8),
            pltpu.VMEM((GROUP * K, CHUNK), F8),
            pltpu.VMEM((2, QN, LANES), jnp.int32),
        ],
        compiler_params=PARAMS,
        name="score",
    )(where, limits, words, *tabs)


def merge(lists):
    return pl.pallas_call(
        merge_kernel,
        out_shape=(
            jax.ShapeDtypeStruct((QB, LANES), jnp.int32),
            jax.ShapeDtypeStruct((1, QB), jnp.int32),
        ),
        in_specs=[VMEM],
        out_specs=(VMEM, VMEM),
        compiler_params=PARAMS,
        name="merge",
    )(lists)


def per_device(codes, tables, limits):
    where = jnp.stack([lax.axis_index("db"), lax.axis_index("sub")]).astype(jnp.int32)
    shifted = [
        lax.ppermute(tables, "sub", [(x, (x + k) % PARTS) for x in range(PARTS)])
        for k in range(1, PARTS)
    ]
    sent = pack(codes).reshape(RANGES * PARTS, 8, LANES)
    words = lax.all_to_all(sent, ("db", "sub"), split_axis=0, concat_axis=0, tiled=True)
    lists = score(where, limits.reshape(16, LANES), words, [tables] + shifted)
    received = lax.all_to_all(lists, "sub", split_axis=0, concat_axis=0, tiled=True)
    ids, count = merge(received)
    return ids, count.reshape(QB)


def solution(mesh):
    placed = (P("db", "sub"), P("db", "sub", None), P())
    return jax.shard_map(
        per_device,
        mesh=mesh,
        in_specs=placed,
        out_specs=(P(("db", "sub"), None), P(("db", "sub"))),
        check_vma=False,
    )
```

time: 276 us -> 72.8 us (0.26); the launches traced: 273 us -> 72.5 us
  other arithmetic: 92.4 us -> 0.08 us
  waiting for transfers between devices: 56.8 us -> 21.2 us
  matrix products: 35 us -> 0 us
  local copies, waits for them, and re-layouts: 34.7 us -> 1.04 us
  Pallas kernels: 0 us -> 24.9 us
  blocking collectives: 29.4 us -> 9.6 us
  between operations: 14.3 us -> 0.69 us
  starting transfers between devices: 8.94 us -> 15 us
    reduce_sum x34 -> x0, other arithmetic: 77.1 us -> none  [the longest x32 76.4 us: list_hits(): jnp.sum(jnp.where(equal, position[None, None, :], 0), axis=2, dtype=jnp.i...]
    all_gather x1 -> x0, waiting for transfers between devices: 50.5 us -> none  [per_device(): query_tables = lax.all_gather(own_queries, 'db', axis=0, tiled=True)]
    dot_general x5 -> x0, matrix products: 35 us -> none  [the longest x4 31.4 us: per_device(): jnp.dot(query_tables[:, group * span:(group + 1) * span], encoded, prefer...]
    eq x32 -> x0, local copies, waits for them, and re-layouts: 27.2 us -> none  [list_hits(): running_block[:, None, :] == wanted_block[:, :, None] + 1.0]
    pallas_call x0 -> x3, Pallas kernels: none -> 24.9 us  [the longest x1 22.4 us: score(): pl.pallas_call(score_kernel, out_shape=jax.ShapeDtypeStruct((QN, 2 * LANE...]
    all_to_all x2 -> x1, blocking collectives: 29.4 us -> 9.6 us  [per_device(): lax.all_to_all(lists, 'sub', split_axis=0, concat_axis=0, tiled=True)]
    all_to_all x2 -> x1, waiting for transfers between devices: 6.35 us -> 21.2 us  [per_device(): lax.all_to_all(sent, ('db', 'sub'), split_axis=0, concat_axis=0, tiled=True)]
    eq x1 -> x0, other arithmetic: 12.1 us -> none  [one_hot_codes(): table = group_codes.T[:, None, :] == centroid[None, :, None]]
  transfers between devices with their start and end apart: 3 -> 4, of which waited for: 3 -> 1; matrix products, arithmetic and copies ran while one was open for 7% -> 2% of each run, Pallas kernels for 0% -> 1%
where the time goes in v1:
time: 72.8 us; the launch traced here: 72.5 us
  Pallas kernels  24.9 us (34%)
  waiting for transfers between devices  21.2 us (29%)
  starting transfers between devices  15 us (21%)
  blocking collectives  9.6 us (13%)
  local copies, waits for them, and re-layouts  1.04 us (1%)
    pallas_call x1, Pallas kernels, score(): pl.pallas_call(score_kernel, out_shape=jax.ShapeDtypeStruct((QN, 2 * LANE...  22.4 us
    all_to_all x1, waiting for transfers between devices, per_device(): lax.all_to_all(sent, ('db', 'sub'), split_axis=0, concat_axis=0, tiled=True)  21.2 us
    all_to_all x1, blocking collectives, per_device(): lax.all_to_all(lists, 'sub', split_axis=0, concat_axis=0, tiled=True)  9.6 us
    all_to_all x1, starting transfers between devices, per_device(): lax.all_to_all(sent, ('db', 'sub'), split_axis=0, concat_axis=0, tiled=True)  8.6 us
    ppermute x3, starting transfers between devices, per_device(): lax.ppermute(tables, 'sub', [(x, (x + k) % PARTS) for x in range(PARTS)])  6.42 us
    pallas_call x1, Pallas kernels, merge(): pl.pallas_call(merge_kernel, out_shape=(jax.ShapeDtypeStruct((QB, LANES),...  1.46 us
  transfers between devices with their start and end apart: 4, of which 1 were waited for; matrix products, arithmetic and copies ran while one was open for 2% of the time, Pallas kernels for 1%

profile of v1, /device:TPU:0, one launch (start us, length us, event | category | flops | bytes accessed | tf_op | source)
XLA Modules:
  0.0 72.5 jit_solution(12790845244524536623)
XLA Ops:
  0.6 3.2 %collective-permute-start.1 = (bf16[64,16,256]{2,1,0:T(8,128)(2,1)}, bf16[64,16,256]{2,1,0:T(8,128)(2,1)S(1)}, u32[]{:S(2)}, u32[]{:S(2)}) collective-permute-start(bf16[64,16,256]{2,1,0:T(8,128)(2,1)} %t0.1), channel_id=1, source_target_pairs={{0,2},{1,3},{2,0},{3,1},{4,6},{5,7},{6,4},{7,5},{8,10},{9,11},{10,... | collective-permute-start | bytes 1572872 | tf_op jit(solution)/shard_map/ppermute | solution.py:286
  3.8 0.6 collective-permute-start
  4.4 2.6 %collective-permute-start.2 = (bf16[64,16,256]{2,1,0:T(8,128)(2,1)}, bf16[64,16,256]{2,1,0:T(8,128)(2,1)S(1)}, u32[]{:S(2)}, u32[]{:S(2)}) collective-permute-start(bf16[64,16,256]{2,1,0:T(8,128)(2,1)} %t0.1), channel_id=1, source_target_pairs={{0,3},{1,0},{2,1},{3,2},{4,7},{5,4},{6,5},{7,6},{8,11},{9,8},{10,9... | collective-permute-start | bytes 1572872 | tf_op jit(solution)/shard_map/ppermute | solution.py:286
  7.1 1.0 %copy.5.codes_ref = s32[1024,16]{1,0:T(8,128)S(1)} copy(s32[1024,16]{0,1:T(8,128)} %param.3) | data formatting | bytes 131072 | tf_op args[0]
  8.1 1.0 %pack.1 = s32[32,32,128]{2,1,0:T(8,128)} custom-call(s32[1024,16]{1,0:T(8,128)S(1)} %copy.5.codes_ref), custom_call_target="tpu_custom_call" | custom-call | tf_op jit(solution)/shard_map/pack/pallas_call | solution.py:242
  9.1 0.0 copy-start
  9.1 8.6 %all-to-all-start = ((s32[128,8,128]{2,1,0:T(8,128)}), s32[128,8,128]{2,1,0:T(8,128)S(1)}, u32[]{:S(2)}, u32[]{:S(2)}) async-start(s32[128,8,128]{2,1,0:T(8,128)} %bitcast.3), calls=%async_computation | async-start | bytes 1048576 | tf_op jit(solution)/shard_map/all_to_all | solution.py:290
  17.7 0.0 copy-start.1
  17.7 0.1 pad_add_fusion.where_ref
  17.8 21.2 %all-to-all-done.words_ref = s32[128,8,128]{2,1,0:T(8,128)S(1)} async-done(((s32[128,8,128]{2,1,0:T(8,128)}), s32[128,8,128]{2,1,0:T(8,128)S(1)}, u32[]{:S(2)}, u32[]{:S(2)}) %all-to-all-start) | async-done | bytes 524320 | tf_op jit(solution)/shard_map/all_to_all | solution.py:290
  39.0 0.0 collective-permute-done.1.t2
  39.0 0.0 collective-permute-done.t1
  39.0 0.0 collective-permute-done.2.t3
  39.0 0.0 copy-done
  39.0 0.0 copy-done.1
  39.0 22.4 %score.1 = s32[64,256]{1,0:T(8,128)S(1)} custom-call(s32[2]{0:T(128)S(1)} %pad_add_fusion.where_ref, s32[16,128]{1,0:T(8,128)S(1)} %bitcast.9, s32[128,8,128]{2,1,0:T(8,128)S(1)} %all-to-all-done.words_ref, bf16[64,16,256]{2,1,0:T(8,128)(2,1)S(1)} %copy-done, bf16[64,16,256]{2,1,0:T(8,128)(2,1)S(1)} %collective-permute-done.t1, ...), custom_call_target="tpu_custom_call" | custom-call | tf_op jit(solution)/shard_map/score/pallas_call | solution.py:253
  61.5 9.6 %all_to_all.16 = s32[4,16,256]{2,1,0:T(8,128)S(1)} all-to-all(s32[4,16,256]{2,1,0:T(8,128)S(1)} %bitcast.7), channel_id=1, replica_groups=mesh['db'=32,'sub'=4] {'sub'}, dimensions={0} | all-to-all | bytes 131072 | tf_op jit(solution)/shard_map/all_to_all | solution.py:292
  71.1 1.5 %merge.1 = (s32[16,128]{1,0:T(8,128)}, s32[1,16]{1,0:T(1,128)}) custom-call(s32[64,256]{1,0:T(8,128)S(1)} %bitcast.8), custom_call_target="tpu_custom_call" | custom-call | tf_op jit(solution)/shard_map/merge/pallas_call | solution.py:270
Async XLA Ops:
  0.6 38.4 %collective-permute-start.1 = (bf16[64,16,256]{2,1,0:T(8,128)(2,1)}, bf16[64,16,256]{2,1,0:T(8,128)(2,1)S(1)}, u32[]{:S(2)}, u32[]{:S(2)}) collective-permute-start(bf16[64,16,256]{2,1,0:T(8,128)(2,1)} %t0.1), channel_id=1, source_target_pairs={{0,2},{1,3},{2,0},{3,1},{4,6},{5,7},{6,4},{7,5},{8,10},{9,11},{10,... | collective-permute-start | bytes 1572872 | tf_op jit(solution)/shard_map/ppermute | solution.py:286
  3.8 35.2 %collective-permute-start = (bf16[64,16,256]{2,1,0:T(8,128)(2,1)}, bf16[64,16,256]{2,1,0:T(8,128)(2,1)S(1)}, u32[]{:S(2)}, u32[]{:S(2)}) collective-permute-start(bf16[64,16,256]{2,1,0:T(8,128)(2,1)} %t0.1), channel_id=1, source_target_pairs={{0,1},{1,2},{2,3},{3,0},{4,5},{5,6},{6,7},{7,4},{8,9},{9,10},{10,1... | collective-permute-start | bytes 1572872 | tf_op jit(solution)/shard_map/ppermute | solution.py:286
  4.4 34.6 %collective-permute-start.2 = (bf16[64,16,256]{2,1,0:T(8,128)(2,1)}, bf16[64,16,256]{2,1,0:T(8,128)(2,1)S(1)}, u32[]{:S(2)}, u32[]{:S(2)}) collective-permute-start(bf16[64,16,256]{2,1,0:T(8,128)(2,1)} %t0.1), channel_id=1, source_target_pairs={{0,3},{1,0},{2,1},{3,2},{4,7},{5,4},{6,5},{7,6},{8,11},{9,8},{10,9... | collective-permute-start | bytes 1572872 | tf_op jit(solution)/shard_map/ppermute | solution.py:286
  9.1 29.9 %copy-start = (bf16[64,16,256]{2,1,0:T(8,128)(2,1)S(1)}, bf16[64,16,256]{2,1,0:T(8,128)(2,1)}, u32[]{:S(2)}) copy-start(bf16[64,16,256]{2,1,0:T(8,128)(2,1)} %t0.1) | copy-start | bytes 1572868
  9.1 29.9 %all-to-all-start = ((s32[128,8,128]{2,1,0:T(8,128)}), s32[128,8,128]{2,1,0:T(8,128)S(1)}, u32[]{:S(2)}, u32[]{:S(2)}) async-start(s32[128,8,128]{2,1,0:T(8,128)} %bitcast.3), calls=%async_computation | async-start | bytes 1048576 | tf_op jit(solution)/shard_map/all_to_all | solution.py:290
  17.7 21.3 %copy-start.1 = (s32[2048]{0:T(1024)S(1)}, s32[2048]{0:T(1024)}, u32[]{:S(2)}) copy-start(s32[2048]{0:T(1024)} %param.5) | copy-start | bytes 24580
